TPU v7x, 32 devices: a whole 2x2x4 slice. The times are simulated.
32 devices in a mesh: chan: 8 (over z, x), tile: 4 (over y, core).
Axes of the slice: x: 2, y: 2, z: 4, core: 2. Of those that a mesh axis runs over, the one named last changes fastest.
Arguments:
- voltages: bfloat16 [2, 1024, 5888], P(None, 'chan'), may hold values from -6 to 6
- taps: float32 [16, 256], replicated, may hold values from -0.09375 to 0.09375
- beam_weights: bfloat16 [2, 256, 64, 1024], P(None, 'chan'), may hold values from -0.1875 to 0.1875
- station_masks: int32 [64, 512], replicated, may hold values 0 or 1
- tile_pairs: int32 [36, 2], P('tile'), may hold values from 0 to 7, as said below
Outputs:
- visibilities: float32 [2, 256, 36, 128, 128], P(None, 'chan', 'tile')
- beams: bfloat16 [2, 64, 8, 256], P(None, 'tile', 'chan')
Inputs may be any that keep to these rules, and one draw needn't show every extreme that they name: `tile_pairs`: each pair (r, s) with 0 <= s <= r < 8 stands in exactly one row, r in the first column and s in the second.
All inputs are finite; a program needn't handle non-finite values.
Results may differ from a plain program's by a relative error of at most 0.0049.
Values may be sent and summed in bfloat16 or wider, within the bound.
A program may use at most 128 MiB of HBM per device.

v0:
```python
import math
import jax
import jax.numpy as jnp
from jax import lax
from jax.sharding import PartitionSpec as P

TB = 128


def dft_table(channels):
    counter = jnp.arange(channels, dtype=jnp.int32)
    wrapped = counter[:, None] * counter[None, :] % channels
    phases = 2.0 * math.pi / channels * wrapped.astype(jnp.float32)
    cosine = jnp.cos(phases)
    sine_part = jnp.sin(phases)
    first_row = jnp.stack([cosine, sine_part], axis=1)
    second_row = jnp.stack([-sine_part, cosine], axis=1)
    return jnp.stack([first_row, second_row], axis=1)


def filterbank(voltages, taps, count):
    taps_count, channels = taps.shape
    in_dev = voltages.shape[1]
    framed = voltages.reshape(2, in_dev, count + taps_count - 1, channels)
    frames = jnp.zeros((2, in_dev, count, channels), jnp.float32)
    for tap_index in range(taps_count):
        frames = frames + taps[tap_index] * framed[:, :, tap_index : tap_index + count, :].astype(
            jnp.float32
        )
    spectra = jnp.einsum(
        "crsk,sitk->crit",
        dft_table(channels),
        frames,
        precision=lax.Precision.HIGHEST,
        preferred_element_type=jnp.float32,
    )
    return spectra.astype(jnp.bfloat16)


def correlate(time_piece, tile_pairs):
    chan_dev = time_piece.shape[0]
    inputs = time_piece.shape[2]
    time_width = time_piece.shape[3]
    blocks = time_piece.reshape(chan_dev, 2, inputs // TB, TB, time_width)
    left_rows = jnp.take(blocks, tile_pairs[:, 0], axis=2)
    right_rows = jnp.take(blocks, tile_pairs[:, 1], axis=2)
    rotated = jnp.stack([left_rows[:, 1], -left_rows[:, 0]], axis=1)
    stacked = jnp.stack([left_rows, rotated], axis=0)
    return jnp.einsum(
        "ocrkaw,crkbw->ockab", stacked, right_rows, preferred_element_type=jnp.float32
    )


def beamform(own_time, beam_weights, station_masks):
    beams_count, stations = station_masks.shape
    live_inputs = jnp.broadcast_to(station_masks[:, :, None], (beams_count, stations, 2))
    live_inputs = live_inputs.reshape(beams_count, 2 * stations).astype(jnp.bfloat16)
    weights = beam_weights * live_inputs[None, None]
    products = jnp.einsum("scbi,crit->csrbt", weights, own_time, preferred_element_type=jnp.float32)
    real_part = products[:, 0, 0] - products[:, 1, 1]
    imag_part = products[:, 0, 1] + products[:, 1, 0]
    return jnp.transpose(jnp.stack([real_part, imag_part]), (0, 2, 3, 1)).astype(jnp.bfloat16)


def on_device(voltages, taps, beam_weights, station_masks, tile_pairs):
    taps_count, channels = taps.shape
    tile_count = lax.axis_size("tile")
    total_time = voltages.shape[2] // channels - taps_count + 1
    quarter = total_time // tile_count
    tile_index = lax.axis_index("tile")
    spectra = filterbank(voltages, taps, total_time)
    turned = lax.all_to_all(spectra, "chan", split_axis=0, concat_axis=2, tiled=True)
    own_time = lax.dynamic_slice_in_dim(turned, tile_index * quarter, quarter, 3)
    visibility = correlate(turned, tile_pairs)
    visibility = visibility * (1.0 / total_time)
    beam_part = beamform(own_time, beam_weights, station_masks)
    beams = lax.all_to_all(
        lax.all_to_all(beam_part, "tile", split_axis=1, concat_axis=2, tiled=True),
        "chan",
        split_axis=2,
        concat_axis=3,
        tiled=True,
    )
    return (visibility, beams)


def solution(mesh):
    in_specs = (P(None, "chan", None), P(), P(None, "chan", None, None), P(), P("tile", None))
    out_specs = (P(None, "chan", "tile", None, None), P(None, "tile", "chan", None))
    return jax.shard_map(
        on_device, mesh=mesh, in_specs=in_specs, out_specs=out_specs, check_vma=False
    )
```

profile of v0, /device:TPU:0, one launch (start us, length us, event | category | flops | bytes accessed | tf_op | source)
XLA Modules:
  0.0 124.9 jit_solution(12216933234083120169)
XLA Ops:
  0.6 1.0 fusion.109
  1.6 1.7 %fusion.107 = (f32[256,1,256]{2,0,1:T(8,128)S(1)}, f32[256,1,256]{2,0,1:T(8,128)}) fusion(), kind=kLoop, calls=%fused_computation.119 | loop fusion | flops 917504 | bytes 524288 | tf_op jit(solution)/shard_map/sin | solution.py:15
  3.3 1.7 %fusion.119 = (f32[1,256]{1,0:T(1,128)S(1)}, f32[1,256]{1,0:T(1,128)S(1)}, f32[1,256]{1,0:T(1,128)S(1)}, f32[1,256]{1,0:T(1,128)S(1)}, f32[1,256]{1,0:T(1,128)},...) fusion(f32[16,256]{1,0:T(8,128)} %param.8), kind=kLoop, calls=%fused_computation.141 | loop fusion | bytes 32768 | tf_op jit(solution)/shard_map/slice | solution.py:27
  5.0 3.5 %copy.96 = bf16[2,128,5888]{1,2,0:T(8,128)(2,1)S(1)} copy(bf16[2,128,5888]{2,1,0:T(8,128)(2,1)} %param.7) | data formatting | bytes 6029312 | tf_op args[0]
  8.5 1.1 maximum_bitcast_fusion.1
  9.6 7.1 %bitcast_convert_fusion = bf16[256,2,128,8]{2,0,3,1:T(8,128)(2,1)S(1)} fusion(bf16[2,128,23,256]{1,3,2,0:T(8,128)(2,1)S(1)} %bitcast.122, f32[256,1,2,256]{3,0,2,1:T(8,128)S(1)} %get-tuple-element.26, f32[256,1,2,256]{3,0,2,1:T(8,128)S(1)} %get-tuple-element.25, f32[256]{0:T(256)} %bitcast.145, f32[256]{0:T(256)} %bitcast.146, f32[256]{0:T(256)S(1)} %bitcast.132, ...), kind=kOutput, calls=%fused_computation.10 | convolution fusion | flops 3246653440 | bytes 18890752 | tf_op jit(solution)/shard_map/crsk,sitk->crit/dot_general | solution.py:30
  16.7 1.6 %copy.98 = bf16[256,2,128,8]{2,3,1,0:T(8,128)(2,1)} copy(bf16[256,2,128,8]{2,0,3,1:T(8,128)(2,1)S(1)} %bitcast_convert_fusion) | data formatting | bytes 2097152 | tf_op jit(solution)/shard_map/convert_element_type | solution.py:37
  18.4 7.4 %all-to-all-start = ((bf16[256,2,128,8]{2,3,1,0:T(8,128)(2,1)}), bf16[256,2,128,8]{2,3,1,0:T(8,128)(2,1)S(1)}, u32[]{:S(2)}, u32[]{:S(2)}) async-start(bf16[256,2,128,8]{2,3,1,0:T(8,128)(2,1)} %copy.98), calls=%async_computation | async-start | bytes 2097152 | tf_op jit(solution)/shard_map/all_to_all | solution.py:72
  26.2 25.3 %all-to-all-done = bf16[256,2,128,8]{2,3,1,0:T(8,128)(2,1)S(1)} async-done(((bf16[256,2,128,8]{2,3,1,0:T(8,128)(2,1)}), bf16[256,2,128,8]{2,3,1,0:T(8,128)(2,1)S(1)}, u32[]{:S(2)}, u32[]{:S(2)}) %all-to-all-start) | async-done | bytes 1048608 | tf_op jit(solution)/shard_map/all_to_all | solution.py:72
  51.5 0.3 copy.144
  51.8 6.9 %fusion.58 = f32[32,2,2,64,2]{3,4,1,2,0:T(2,128)S(1)} fusion(bf16[32,2,1024,8]{2,3,1,0:T(8,128)(2,1)S(1)} %bitcast.118, s32[]{:T(128)S(6)} %select_n.39, bf16[2,32,64,1024]{3,2,1,0:T(8,128)(2,1)} %param.9, bf16[64,1024]{1,0:T(8,128)(2,1)S(1)} %copy.104), kind=kOutput, calls=%fused_computation.64 | convolution fusion | flops 37748736 | bytes 8847364 | tf_op jit(solution)/shard_map/scbi,crit->csrbt/dot_general | solution.py:59
  58.9 0.7 reshape.184
  59.7 3.3 %all-to-all-start.1 = ((bf16[4,2,1024]{2,1,0:T(2,128)(2,1)}), bf16[4,2,1024]{2,1,0:T(2,128)(2,1)S(1)}, u32[]{:S(2)}, u32[]{:S(2)}) async-start(bf16[4,2,1024]{2,1,0:T(2,128)(2,1)} %reshape.184), calls=%async_computation.1 | async-start | bytes 32768 | tf_op jit(solution)/shard_map/all_to_all | solution.py:78
  62.9 1.0 gather_fusion.1
  63.9 1.2 fusion.97
  65.1 0.2 fusion.118
  65.3 0.2 maximum_bitcast_fusion
  65.5 1.0 gather_fusion
  66.5 0.2 all-to-all-done.1
  66.9 0.7 reshape.186
  67.6 3.6 %all-to-all-start.2 = ((bf16[8,2,512]{2,1,0:T(2,128)(2,1)}), bf16[8,2,512]{2,1,0:T(2,128)(2,1)S(1)}, u32[]{:S(2)}, u32[]{:S(2)}) async-start(bf16[8,2,512]{2,1,0:T(2,128)(2,1)} %reshape.186), calls=%async_computation.2 | async-start | bytes 32768 | tf_op jit(solution)/shard_map/all_to_all | solution.py:77
  71.2 16.0 %fusion = f32[2,32,9,128,128]{3,4,0,2,1:T(8,128)} fusion(bf16[1,32,2,9,128,8]{4,5,2,0,3,1:T(8,128)(2,1)S(1)} %maximum_bitcast_fusion, bf16[1,32,2,9,128,8]{4,5,2,0,3,1:T(8,128)(2,1)} %get-tuple-element.19, bf16[9,32,2,128,8]{3,4,2,1,0:T(8,128)(2,1)S(1)} %gather_fusion, pred[9]{0:T(512)(128)(4,1)S(1)} %get-tuple-element.15), kind=kOutput, calls=%fused_computation.3 | convolution fusion | flops 316735488 | bytes 41287688 | tf_op jit(solution)/shard_map/ocrkaw,crkbw->ockab/dot_general | solution.py:49
  87.2 36.9 %copy.113 = f32[2,32,9,128,128]{4,3,2,1,0:T(8,128)} copy(f32[2,32,9,128,128]{3,4,0,2,1:T(8,128)} %fusion) | data formatting | bytes 75497472
  124.2 0.7 all_to_all.44
  (21 shorter events, 0.9 us)
Async XLA Ops:
  16.7 9.1 %copy-start = (s32[64,512]{1,0:T(8,128)S(1)}, s32[64,512]{1,0:T(8,128)}, u32[]{:S(2)}) copy-start(s32[64,512]{1,0:T(8,128)} %param.10) | copy-start | bytes 393220
  18.4 7.8 %copy-start.1 = (s32[9,2]{0,1:T(2,128)S(1)}, s32[9,2]{0,1:T(2,128)}, u32[]{:S(2)}) copy-start(s32[9,2]{0,1:T(2,128)} %param.11) | copy-start | bytes 220
  18.4 33.2 %all-to-all-start = ((bf16[256,2,128,8]{2,3,1,0:T(8,128)(2,1)}), bf16[256,2,128,8]{2,3,1,0:T(8,128)(2,1)S(1)}, u32[]{:S(2)}, u32[]{:S(2)}) async-start(bf16[256,2,128,8]{2,3,1,0:T(8,128)(2,1)} %copy.98), calls=%async_computation | async-start | bytes 2097152 | tf_op jit(solution)/shard_map/all_to_all | solution.py:72
  59.7 7.1 %all-to-all-start.1 = ((bf16[4,2,1024]{2,1,0:T(2,128)(2,1)}), bf16[4,2,1024]{2,1,0:T(2,128)(2,1)S(1)}, u32[]{:S(2)}, u32[]{:S(2)}) async-start(bf16[4,2,1024]{2,1,0:T(2,128)(2,1)} %reshape.184), calls=%async_computation.1 | async-start | bytes 32768 | tf_op jit(solution)/shard_map/all_to_all | solution.py:78
  67.6 56.5 %all-to-all-start.2 = ((bf16[8,2,512]{2,1,0:T(2,128)(2,1)}), bf16[8,2,512]{2,1,0:T(2,128)(2,1)S(1)}, u32[]{:S(2)}, u32[]{:S(2)}) async-start(bf16[8,2,512]{2,1,0:T(2,128)(2,1)} %reshape.186), calls=%async_computation.2 | async-start | bytes 32768 | tf_op jit(solution)/shard_map/all_to_all | solution.py:77
where the time goes:
time: 126 us; the launch traced here: 125 us
  local copies, waits for them, and re-layouts  48.9 us (39%)
  matrix products  29.9 us (24%)
  waiting for transfers between devices  25.5 us (20%)
  starting transfers between devices  14.2 us (11%)
  other arithmetic  5.54 us (4%)
    unnamed x10, local copies, waits for them, and re-layouts  42 us
    all_to_all x1, waiting for transfers between devices, on_device(): lax.all_to_all(spectra, 'chan', split_axis=0, concat_axis=2, tiled=True)  25.3 us
    dot_general x1, matrix products, correlate(): jnp.einsum('ocrkaw,crkbw->ockab', stacked, right_rows, preferred_element_...  16 us
    all_to_all x1, starting transfers between devices, on_device(): lax.all_to_all(spectra, 'chan', split_axis=0, concat_axis=2, tiled=True)  7.38 us
    dot_general x1, matrix products, filterbank(): jnp.einsum('crsk,sitk->crit', dft_table(channels), frames, precision=lax....  7.12 us
    dot_general x1, matrix products, beamform(): jnp.einsum('scbi,crit->csrbt', weights, own_time, preferred_element_type=...  6.86 us
    all_to_all x1, starting transfers between devices, on_device(): lax.all_to_all(lax.all_to_all(beam_part, 'tile', split_axis=1, concat_axi...  3.59 us
    all_to_all x1, starting transfers between devices, on_device(): lax.all_to_all(beam_part, 'tile', split_axis=1, concat_axis=2, tiled=True)  3.25 us
  transfers between devices with their start and end apart: 3, of which 2 were waited for; matrix products, arithmetic and copies ran while one was open for 46% of the time, Pallas kernels for 0%

commit v1 on v0

--- a/solution.py
+++ b/solution.py
@@ -69,7 +69,10 @@
     quarter = total_time // tile_count
     tile_index = lax.axis_index("tile")
     spectra = filterbank(voltages, taps, total_time)
-    turned = lax.all_to_all(spectra, "chan", split_axis=0, concat_axis=2, tiled=True)
+    turned = jnp.concatenate(
+        lax.all_to_all(jnp.stack(jnp.split(spectra, lax.axis_size("chan"), axis=0)), "chan", 0, 0),
+        axis=2,
+    )
     own_time = lax.dynamic_slice_in_dim(turned, tile_index * quarter, quarter, 3)
     visibility = correlate(turned, tile_pairs)
     visibility = visibility * (1.0 / total_time)

time: 126 us -> 131 us (1.040)
  local copies, waits for them, and re-layouts: 48.9 us -> 55.5 us
    unnamed x10 -> x21, local copies, waits for them, and re-layouts: 42 us -> 48.4 us
    convert_element_type x1 -> x0, local copies, waits for them, and re-layouts: 1.65 us -> none  [filterbank(): return spectra.astype(jnp.bfloat16)]
    all_to_all x3, local copies, waits for them, and re-layouts: 0.02 us -> 1.49 us  [on_device(): lax.all_to_all(beam_part, 'tile', split_axis=1, concat_axis=2, tiled=True)]
  transfers between devices with their start and end apart: 3 -> 3, of which waited for: 2 -> 2; matrix products, arithmetic and copies ran while one was open for 46% -> 43% of each run, Pallas kernels for 0% -> 0%
where the time goes in v1:
time: 131 us; the launch traced here: 130 us
  local copies, waits for them, and re-layouts  55.5 us (42%)
  matrix products  28.7 us (22%)
  waiting for transfers between devices  25.1 us (19%)
  starting transfers between devices  14.1 us (11%)
  other arithmetic  5.99 us (5%)
    unnamed x21, local copies, waits for them, and re-layouts  48.4 us
    all_to_all x1, waiting for transfers between devices, on_device(): lax.all_to_all(jnp.stack(jnp.split(spectra, lax.axis_size('chan'), axis=0...  24.1 us
    dot_general x1, matrix products, correlate(): jnp.einsum('ocrkaw,crkbw->ockab', stacked, right_rows, preferred_element_...  14.8 us
    all_to_all x1, starting transfers between devices, on_device(): lax.all_to_all(jnp.stack(jnp.split(spectra, lax.axis_size('chan'), axis=0...  7.26 us
    dot_general x1, matrix products, filterbank(): jnp.einsum('crsk,sitk->crit', dft_table(channels), frames, precision=lax....  7.13 us
    dot_general x1, matrix products, beamform(): jnp.einsum('scbi,crit->csrbt', weights, own_time, preferred_element_type=...  6.84 us
    all_to_all x1, starting transfers between devices, on_device(): lax.all_to_all(lax.all_to_all(beam_part, 'tile', split_axis=1, concat_axi...  3.59 us
    all_to_all x1, starting transfers between devices, on_device(): lax.all_to_all(beam_part, 'tile', split_axis=1, concat_axis=2, tiled=True)  3.25 us
  transfers between devices with their start and end apart: 3, of which 2 were waited for; matrix products, arithmetic and copies ran while one was open for 43% of the time, Pallas kernels for 0%

profile of v1, /device:TPU:0, one launch (start us, length us, event | category | flops | bytes accessed | tf_op | source)
XLA Modules:
  0.0 130.3 jit_solution(9184726608319622639)
XLA Ops:
  0.6 1.0 fusion.115
  1.6 1.7 %fusion.113 = (f32[256,1,256]{2,0,1:T(8,128)S(1)}, f32[256,1,256]{2,0,1:T(8,128)}) fusion(), kind=kLoop, calls=%fused_computation.133 | loop fusion | flops 917504 | bytes 524288 | tf_op jit(solution)/shard_map/sin | solution.py:15
  3.3 1.7 %fusion.124 = (f32[1,256]{1,0:T(1,128)S(1)}, f32[1,256]{1,0:T(1,128)S(1)}, f32[1,256]{1,0:T(1,128)S(1)}, f32[1,256]{1,0:T(1,128)S(1)}, f32[1,256]{1,0:T(1,128)},...) fusion(f32[16,256]{1,0:T(8,128)} %param.8), kind=kLoop, calls=%fused_computation.154 | loop fusion | bytes 32768 | tf_op jit(solution)/shard_map/slice | solution.py:27
  5.0 3.5 %copy.74 = bf16[2,128,5888]{1,2,0:T(8,128)(2,1)S(1)} copy(bf16[2,128,5888]{2,1,0:T(8,128)(2,1)} %param.7) | data formatting | bytes 6029312 | tf_op args[0]
  8.5 1.1 maximum_bitcast_fusion.1
  9.6 7.1 %bitcast_convert_fusion = bf16[256,2,128,8]{2,0,3,1:T(8,128)(2,1)S(1)} fusion(bf16[2,128,23,256]{1,3,2,0:T(8,128)(2,1)S(1)} %bitcast.146, f32[256,1,2,256]{3,0,2,1:T(8,128)S(1)} %get-tuple-element.22, f32[256,1,2,256]{3,0,2,1:T(8,128)S(1)} %get-tuple-element.21, f32[256]{0:T(256)} %bitcast.170, f32[256]{0:T(256)} %bitcast.171, f32[256]{0:T(256)S(1)} %bitcast.157, ...), kind=kOutput, calls=%fused_computation.9 | convolution fusion | flops 3246653440 | bytes 18890752 | tf_op jit(solution)/shard_map/crsk,sitk->crit/dot_general | solution.py:30
  16.8 0.7 fusion.112
  17.4 0.7 fusion.111
  20.7 0.7 fusion.106
  22.1 7.3 %all-to-all-start = ((bf16[8,32,2,128,8]{3,1,4,2,0:T(8,128)(2,1)}), bf16[8,32,2,128,8]{3,1,4,2,0:T(8,128)(2,1)S(1)}, u32[]{:S(2)}, u32[]{:S(2)}) async-start(bf16[8,32,2,128,8]{3,1,4,2,0:T(8,128)(2,1)} %fusion.105), calls=%async_computation | async-start | bytes 2097152 | tf_op jit(solution)/shard_map/all_to_all | solution.py:73
  31.0 24.1 %all-to-all-done = bf16[8,32,2,128,8]{3,1,4,2,0:T(8,128)(2,1)S(1)} async-done(((bf16[8,32,2,128,8]{3,1,4,2,0:T(8,128)(2,1)}), bf16[8,32,2,128,8]{3,1,4,2,0:T(8,128)(2,1)S(1)}, u32[]{:S(2)}, u32[]{:S(2)}) %all-to-all-start) | async-done | bytes 1048608 | tf_op jit(solution)/shard_map/all_to_all | solution.py:73
  55.5 6.8 %fusion.56 = f32[32,2,2,64,2]{3,4,1,2,0:T(2,128)S(1)} fusion(bf16[32,2,1024,8]{2,3,1,0:T(8,128)(2,1)S(1)} %bitcast.148, s32[]{:T(128)S(6)} %select_n.39, bf16[2,32,64,1024]{3,2,1,0:T(8,128)(2,1)} %param.9, bf16[64,1024]{1,0:T(8,128)(2,1)S(1)} %copy.80), kind=kOutput, calls=%fused_computation.63 | convolution fusion | flops 37748736 | bytes 8847364 | tf_op jit(solution)/shard_map/scbi,crit->csrbt/dot_general | solution.py:59
  62.6 0.7 reshape.190
  63.3 3.3 %all-to-all-start.1 = ((bf16[4,2,1024]{2,1,0:T(2,128)(2,1)}), bf16[4,2,1024]{2,1,0:T(2,128)(2,1)S(1)}, u32[]{:S(2)}, u32[]{:S(2)}) async-start(bf16[4,2,1024]{2,1,0:T(2,128)(2,1)} %reshape.190), calls=%async_computation.1 | async-start | bytes 32768 | tf_op jit(solution)/shard_map/all_to_all | solution.py:81
  66.6 0.8 gather_fusion.1
  67.4 0.9 gather_fusion
  69.4 1.0 all-to-all-done.1
  70.4 0.7 reshape.191
  71.1 0.8 copy.85
  72.6 1.6 %reshape.192 = bf16[8,2,512]{2,1,0:T(2,128)(2,1)} reshape(bf16[8,2,16,32]{3,2,1,0:T(8,128)(2,1)} %bitcast.151) | data formatting | bytes 32768
  74.2 3.6 %all-to-all-start.2 = ((bf16[8,2,512]{2,1,0:T(2,128)(2,1)}), bf16[8,2,512]{2,1,0:T(2,128)(2,1)S(1)}, u32[]{:S(2)}, u32[]{:S(2)}) async-start(bf16[8,2,512]{2,1,0:T(2,128)(2,1)} %reshape.192), calls=%async_computation.2 | async-start | bytes 32768 | tf_op jit(solution)/shard_map/all_to_all | solution.py:80
  77.8 14.8 %fusion = f32[2,32,9,128,128]{3,4,0,2,1:T(8,128)} fusion(bf16[2,32,2,9,128,8]{4,1,5,2,3,0:T(8,128)(2,1)S(1)} %pad_maximum_fusion, bf16[32,2,9,128,8,1]{3,0,4,1,2,5:T(8,128)(2,1)S(1)} %select_bitcast_fusion), kind=kOutput, calls=%fused_computation.3 | convolution fusion | flops 311427072 | bytes 41287680 | tf_op jit(solution)/shard_map/ocrkaw,crkbw->ockab/dot_general | solution.py:49
  92.6 36.9 %copy.89 = f32[2,32,9,128,128]{4,3,2,1,0:T(8,128)} copy(f32[2,32,9,128,128]{3,4,0,2,1:T(8,128)} %fusion) | data formatting | bytes 75497472
  129.6 0.7 all_to_all.31
  (34 shorter events, 7.4 us)
Async XLA Ops:
  16.7 12.6 %copy-start = (s32[64,512]{1,0:T(8,128)S(1)}, s32[64,512]{1,0:T(8,128)}, u32[]{:S(2)}) copy-start(s32[64,512]{1,0:T(8,128)} %param.10) | copy-start | bytes 393220
  20.1 9.7 %copy-start.3 = (s32[9,2]{0,1:T(2,128)S(1)}, s32[9,2]{0,1:T(2,128)}, u32[]{:S(2)}) copy-start(s32[9,2]{0,1:T(2,128)} %param.11) | copy-start | bytes 220
  22.1 33.0 %all-to-all-start = ((bf16[8,32,2,128,8]{3,1,4,2,0:T(8,128)(2,1)}), bf16[8,32,2,128,8]{3,1,4,2,0:T(8,128)(2,1)S(1)}, u32[]{:S(2)}, u32[]{:S(2)}) async-start(bf16[8,32,2,128,8]{3,1,4,2,0:T(8,128)(2,1)} %fusion.105), calls=%async_computation | async-start | bytes 2097152 | tf_op jit(solution)/shard_map/all_to_all | solution.py:73
  63.3 7.1 %all-to-all-start.1 = ((bf16[4,2,1024]{2,1,0:T(2,128)(2,1)}), bf16[4,2,1024]{2,1,0:T(2,128)(2,1)S(1)}, u32[]{:S(2)}, u32[]{:S(2)}) async-start(bf16[4,2,1024]{2,1,0:T(2,128)(2,1)} %reshape.190), calls=%async_computation.1 | async-start | bytes 32768 | tf_op jit(solution)/shard_map/all_to_all | solution.py:81
  67.3 0.9 copy-start.2
  68.3 0.6 copy-start.1
  74.2 55.3 %all-to-all-start.2 = ((bf16[8,2,512]{2,1,0:T(2,128)(2,1)}), bf16[8,2,512]{2,1,0:T(2,128)(2,1)S(1)}, u32[]{:S(2)}, u32[]{:S(2)}) async-start(bf16[8,2,512]{2,1,0:T(2,128)(2,1)} %reshape.192), calls=%async_computation.2 | async-start | bytes 32768 | tf_op jit(solution)/shard_map/all_to_all | solution.py:80
